TPU v7x, 256 devices: a whole 4x4x8 slice. The times are simulated.
256 devices in a mesh: dp: 8 (over z), slab: 2 (over core), filt: 16 (over y, x).
Axes of the slice: x: 4, y: 4, z: 8, core: 2. Of those that a mesh axis runs over, the one named last changes fastest.
Arguments:
- volume: bfloat16 [512, 16, 128, 128], P('dp', 'slab', 'filt'), parts along dimension 0, may hold values from -6 to 6
- first_weight: bfloat16 [27, 64, 64], replicated, may hold values from -0.15625 to 0.15625
- first_bias: float32 [64], replicated, may hold values from -3 to 3
- second_weight: bfloat16 [27, 64, 64], replicated, may hold values from -0.15625 to 0.15625
- second_bias: float32 [64], replicated, may hold values from -3 to 3
- down_weight: bfloat16 [8, 64, 64], replicated, may hold values from -0.25 to 0.25
- down_bias: float32 [64], replicated, may hold values from -3 to 3
Outputs:
- skip_field: bfloat16 [512, 16, 128, 128], P('dp', 'slab', 'filt'), parts along dimension 0
- coarse_field: bfloat16 [512, 8, 4096], P('dp', 'slab', 'filt'), parts along dimension 0
There are 8 independent parts, one for each index of `dp`. A program takes and returns all parts, laid end to end along the dimension named above; an argument that names none is the same for every part. Nothing has to cross between parts.
All inputs are finite; a program needn't handle non-finite values.
Results may differ from a plain program's by a relative error of at most 0.0052.
Values may be sent and summed in bfloat16 or wider, within the bound.
No kernel may reach another device: no remote copies, remote signals or barrier semaphores. Data moves between devices by JAX's collectives and lax.ppermute only.
A program may use at most 64 MiB of HBM per device.

v0:
```python
import jax
import jax.numpy as jnp
from jax import lax
from jax.sharding import PartitionSpec as P


def extended(shard, sides, width):
    for axis, dim in sides:
        peers, length = (lax.axis_size(axis), shard.shape[dim])
        up = [(i, (i + 1) % peers) for i in range(peers)]
        down = [(j, i) for i, j in up]
        last = lax.slice_in_dim(shard, length - width, length, axis=dim)
        initial = lax.slice_in_dim(shard, 0, width, axis=dim)
        before = lax.ppermute(last, axis, up)
        after = lax.ppermute(initial, axis, down)
        shard = jnp.concatenate([before, shard, after], axis=dim)
    return shard


def leaky_relu(values):
    return jnp.where(values > 0, values, 0.01 * values)


def wrap_cells(source_block, rim_width):
    return jnp.concatenate(
        [source_block[..., -rim_width:], source_block, source_block[..., :rim_width]], axis=3
    )


def fetch_rims(source_block, rim_width):
    padded = extended(source_block, (("slab", 1), ("filt", 2)), rim_width)
    return wrap_cells(padded, rim_width)


def conv_layer(padded, kernel, offsets):
    chans = padded.shape[0]
    stencil = kernel.reshape(3, 3, 3, chans, kernel.shape[2])
    running = lax.conv_general_dilated(
        padded[None],
        stencil,
        (1, 1, 1),
        "VALID",
        dimension_numbers=("NCDHW", "DHWIO", "NCDHW"),
        preferred_element_type=jnp.float32,
    )[0]
    result = leaky_relu(running + offsets[:, None, None, None])
    return result.astype(jnp.bfloat16)


def descend(skip_field, kernel, offsets):
    chans, planes, cells_y, cells_x = skip_field.shape
    stencil = kernel.reshape(2, 2, 2, chans, kernel.shape[2])
    running = lax.conv_general_dilated(
        skip_field[None],
        stencil,
        (2, 2, 2),
        "VALID",
        dimension_numbers=("NCDHW", "DHWIO", "NCDHW"),
        preferred_element_type=jnp.float32,
    )[0]
    result = leaky_relu(running + offsets[:, None, None, None]).astype(jnp.bfloat16)
    return result.reshape(kernel.shape[2], planes // 2, cells_y // 2 * (cells_x // 2))


def per_device(
    volume, first_weight, first_bias, second_weight, second_bias, down_weight, down_bias
):
    hidden = conv_layer(fetch_rims(volume, 1), first_weight, first_bias)
    skip_field = conv_layer(fetch_rims(hidden, 1), second_weight, second_bias)
    coarse_field = descend(skip_field, down_weight, down_bias)
    return (skip_field, coarse_field)


def solution(mesh):
    placed = (P("dp", "slab", "filt", None), P(), P(), P(), P(), P(), P())
    return jax.shard_map(
        per_device,
        mesh=mesh,
        in_specs=placed,
        out_specs=(P("dp", "slab", "filt", None), P("dp", "slab", "filt")),
        check_vma=False,
    )
```

profile of v0, /device:TPU:1, one launch (start us, length us, event | category | flops | bytes accessed | tf_op | source)
XLA Modules:
  0.0 258.5 jit_solution(15687978817819836912)
XLA Ops:
  1.7 3.3 %collective-permute-start = (bf16[64,1,8,128]{3,0,2,1:T(8,128)(2,1)S(1)}, bf16[64,1,8,128]{3,0,2,1:T(8,128)(2,1)S(1)}, u32[]{:S(2)}, u32[]{:S(2)}) collective-permute-start(bf16[64,1,8,128]{3,0,2,1:T(8,128)(2,1)S(1)} %copy.50), channel_id=1, source_target_pairs={{0,16},{16,0},{1,17},{17,1},{2,18},{18,2},{3,19},{19,3},{4,20},{20... | collective-permute-start | bytes 393224 | tf_op jit(solution)/shard_map/ppermute | solution.py:14
  6.0 2.0 constant_dynamic-update-slice_fusion.1
  8.2 4.8 %collective-permute-start.3 = (bf16[64,10,1,128]{3,0,2,1:T(8,128)(2,1)S(1)}, bf16[64,10,1,128]{3,0,2,1:T(8,128)(2,1)S(1)}, u32[]{:S(2)}, u32[]{:S(2)}) collective-permute-start(bf16[64,10,1,128]{3,0,2,1:T(8,128)(2,1)S(1)} %get-tuple-element.15), channel_id=1, source_target_pairs={{1,0},{2,1},{3,2},{4,3},{5,4},{6,5},{7,6},{8,7},{9,8},{10,9},{11,1... | collective-permute-start | bytes 491528 | tf_op jit(solution)/shard_map/ppermute | solution.py:15
  13.0 4.0 %collective-permute-done.2 = bf16[64,10,1,128]{3,0,2,1:T(8,128)(2,1)S(1)} collective-permute-done((bf16[64,10,1,128]{3,0,2,1:T(8,128)(2,1)S(1)}, bf16[64,10,1,128]{3,0,2,1:T(8,128)(2,1)S(1)}, u32[]{:S(2)}, u32[]{:S(2)}) %collective-permute-start.2) | collective-permute-done | bytes 163872 | tf_op jit(solution)/shard_map/ppermute | solution.py:14
  17.8 4.1 %maximum_bitcast_fusion = bf16[64,10,10,1,130]{4,0,2,1,3:T(8,128)(2,1)} fusion(bf16[64,10,10,1]{3,0,2,1:T(8,128)(2,1)S(1)} %get-tuple-element.13, bf16[64,10,1,128]{3,0,2,1:T(8,128)(2,1)S(1)} %collective-permute-done.3, bf16[64,10,8,128]{3,0,2,1:T(8,128)(2,1)S(1)} %constant_dynamic-update-slice_fusion, ...), kind=kLoop, calls=%fused_computation.27 | loop fusion | flops 8320000 | bytes 3328000 | tf_op jit(solution)/shard_map/broadcast_in_dim | solution.py:39
  21.9 5.9 %copy.47 = bf16[64,10,10,1,130]{0,4,2,1,3:T(8,128)(2,1)} copy(bf16[64,10,10,1,130]{4,0,2,1,3:T(8,128)(2,1)} %maximum_bitcast_fusion) | data formatting | bytes 3328000
  27.8 4.5 %pad.clone = bf16[64,10,10,1,136]{0,4,2,1,3:T(8,128)(2,1)} pad(bf16[64,10,10,1,130]{0,4,2,1,3:T(8,128)(2,1)} %copy.47, bf16[]{:T(256)} %constant.1), padding=0_0x0_0x0_0x0_0x0_6 | pad | bytes 3404802 | tf_op jit(solution)/shard_map/broadcast_in_dim | solution.py:39
  32.2 7.1 %reshape.23 = bf16[64,10,10,1,8,17]{0,5,4,2,1,3:T(8,128)(2,1)} reshape(bf16[64,10,10,1,136]{0,4,2,1,3:T(8,128)(2,1)} %pad.clone) | data formatting | bytes 3481600 | tf_op jit(solution)/shard_map/conv_general_dilated | solution.py:38
  39.3 3.1 %copy.29 = bf16[64,10,10,1,8,17]{0,4,5,2,1,3:T(8,128)(2,1)S(1)} copy(bf16[64,10,10,1,8,17]{0,5,4,2,1,3:T(8,128)(2,1)} %reshape.23) | data formatting | bytes 3481600 | tf_op jit(solution)/shard_map/conv_general_dilated | solution.py:38
  42.6 144.2 %broadcast_select_fusion.1 = f32[8,8,8,17,64]{4,2,3,1,0:T(8,128)S(1)} fusion(pred[8,17]{0,1:T(8,128)(4,1)S(1)} %copy-done.7, bf16[3,3,3,64,64]{4,3,2,1,0:T(8,128)(2,1)S(1)} %bitcast.64, bf16[64,10,10,1,7,2]{0,4,5,2,1,3:T(8,128)(2,1)S(1)} %slice.61, bf16[64,10,10,1,8,17]{0,4,5,2,1,3:T(8,128)(2,1)S(1)} %copy.29), kind=kOutput, calls=%fused_computation.38 | convolution fusion | flops 1931579392 | bytes 4369544 | tf_op jit(solution)/shard_map/conv_general_dilated | solution.py:38
  191.7 2.3 fusion.47
  195.3 1.9 copy.32
  197.2 4.8 %collective-permute-start.7 = (bf16[64,10,1,128]{3,0,2,1:T(8,128)(2,1)}, bf16[64,10,1,128]{3,0,2,1:T(8,128)(2,1)S(1)}, u32[]{:S(2)}, u32[]{:S(2)}) collective-permute-start(bf16[64,10,1,128]{3,0,2,1:T(8,128)(2,1)} %copy.32), channel_id=1, source_target_pairs={{1,0},{2,1},{3,2},{4,3},{5,4},{6,5},{7,6},{8,7},{9,8},{10,9},{11,1... | collective-permute-start | bytes 491528 | tf_op jit(solution)/shard_map/ppermute | solution.py:15
  202.0 2.9 %copy.33 = bf16[64,10,8,128]{3,0,2,1:T(8,128)(2,1)} copy(bf16[64,10,8,128]{0,2,3,1:T(8,128)(2,1)S(1)} %pad_maximum_fusion) | data formatting | bytes 2621440 | tf_op jit(solution)/shard_map/concatenate | solution.py:16
  205.5 4.9 %collective-permute-done.6 = bf16[64,10,1,128]{3,0,2,1:T(8,128)(2,1)S(1)} collective-permute-done((bf16[64,10,1,128]{3,0,2,1:T(8,128)(2,1)S(1)}, bf16[64,10,1,128]{3,0,2,1:T(8,128)(2,1)S(1)}, u32[]{:S(2)}, u32[]{:S(2)}) %collective-permute-start.6) | collective-permute-done | bytes 163872 | tf_op jit(solution)/shard_map/ppermute | solution.py:14
  210.4 1.5 pad_maximum_fusion.2
  213.3 4.0 %maximum_bitcast_fusion.1 = bf16[64,10,10,1,130]{4,0,2,1,3:T(8,128)(2,1)} fusion(bf16[64,10,10,1]{3,0,2,1:T(8,128)(2,1)S(1)} %get-tuple-element.11, bf16[64,10,1,128]{3,0,2,1:T(8,128)(2,1)S(1)} %collective-permute-done.7, bf16[64,10,8,128]{3,0,2,1:T(8,128)(2,1)S(1)} %copy-done.1, bf16[64,10,1,128]{3,0,2,1:T(8,128)(2,1)S(1)} %collective-permute-done.6, ...), kind=kLoop, calls=%fused_computation.28 | loop fusion | flops 8320000 | bytes 3328000 | tf_op jit(solution)/shard_map/broadcast_in_dim | solution.py:39
  217.3 5.9 %copy.48 = bf16[64,10,10,1,130]{0,4,2,1,3:T(8,128)(2,1)} copy(bf16[64,10,10,1,130]{4,0,2,1,3:T(8,128)(2,1)} %maximum_bitcast_fusion.1) | data formatting | bytes 3328000
  223.2 4.5 %pad.2.clone = bf16[64,10,10,1,136]{0,4,2,1,3:T(8,128)(2,1)} pad(bf16[64,10,10,1,130]{0,4,2,1,3:T(8,128)(2,1)} %copy.48, bf16[]{:T(256)} %constant.1), padding=0_0x0_0x0_0x0_0x0_6 | pad | bytes 3404802 | tf_op jit(solution)/shard_map/broadcast_in_dim | solution.py:39
  227.6 7.1 %reshape.30 = bf16[64,10,10,1,8,17]{0,5,4,2,1,3:T(8,128)(2,1)} reshape(bf16[64,10,10,1,136]{0,4,2,1,3:T(8,128)(2,1)} %pad.2.clone) | data formatting | bytes 3481600 | tf_op jit(solution)/shard_map/conv_general_dilated | solution.py:38
  234.8 3.1 %copy.36 = bf16[64,10,10,1,8,17]{0,4,5,2,1,3:T(8,128)(2,1)S(1)} copy(bf16[64,10,10,1,8,17]{0,5,4,2,1,3:T(8,128)(2,1)} %reshape.30) | data formatting | bytes 3481600 | tf_op jit(solution)/shard_map/conv_general_dilated | solution.py:38
  238.0 10.0 %fusion.26 = (bf16[8,8,8,17,64]{4,2,3,1,0:T(8,128)(2,1)S(1)}, f32[8,8,8,17,64]{4,2,3,1,0:T(8,128)}) fusion(f32[64]{0:T(128)S(1)} %copy-done.3, pred[8,17]{0,1:T(8,128)(4,1)S(1)} %copy-done.8, bf16[3,3,3,64,64]{4,3,2,1,0:T(8,128)(2,1)S(1)} %bitcast.58, bf16[64,10,10,1,7,2]{0,4,5,2,1,3:T(8,128)(2,1)S(1)} %slice.69, bf16[64,10,10,1,8,17]{0,4,5,2,1,3:T(8,128)(2,1)S(1)} %copy.36), kind=kOutput, calls=%fused_computation.33 | convolution fusion | flops 1934921728 | bytes 5483912 | tf_op jit(solution)/shard_map/conv_general_dilated | solution.py:38
  250.9 3.1 %copy.37 = f32[8,8,8,17,64]{4,1,3,2,0:T(8,128)S(1)} copy(f32[8,8,8,17,64]{4,2,3,1,0:T(8,128)} %get-tuple-element.19) | data formatting | bytes 4456448 | tf_op jit(solution)/shard_map/conv_general_dilated | solution.py:38
  254.7 3.0 %copy.44 = bf16[64,8,8,128]{3,2,1,0:T(8,128)(2,1)} copy(bf16[64,8,8,128]{0,2,3,1:T(8,128)(2,1)S(1)} %fusion.5) | data formatting | bytes 2097152
  (54 shorter events, 15.8 us)
Async XLA Ops:
  0.6 237.3 %copy-start = (bf16[27,64,64]{2,1,0:T(8,128)(2,1)S(1)}, bf16[27,64,64]{2,1,0:T(8,128)(2,1)}, u32[]{:S(2)}) copy-start(bf16[27,64,64]{2,1,0:T(8,128)(2,1)} %param.10) | copy-start | bytes 663556
  1.7 4.3 %collective-permute-start = (bf16[64,1,8,128]{3,0,2,1:T(8,128)(2,1)S(1)}, bf16[64,1,8,128]{3,0,2,1:T(8,128)(2,1)S(1)}, u32[]{:S(2)}, u32[]{:S(2)}) collective-permute-start(bf16[64,1,8,128]{3,0,2,1:T(8,128)(2,1)S(1)} %copy.50), channel_id=1, source_target_pairs={{0,16},{16,0},{1,17},{17,1},{2,18},{18,2},{3,19},{19,3},{4,20},{20... | collective-permute-start | bytes 393224 | tf_op jit(solution)/shard_map/ppermute | solution.py:14
  5.1 3.0 %collective-permute-start.1 = (bf16[64,1,8,128]{3,0,2,1:T(8,128)(2,1)S(1)}, bf16[64,1,8,128]{3,0,2,1:T(8,128)(2,1)S(1)}, u32[]{:S(2)}, u32[]{:S(2)}) collective-permute-start(bf16[64,1,8,128]{3,0,2,1:T(8,128)(2,1)S(1)} %copy.51), channel_id=1, source_target_pairs={{16,0},{0,16},{17,1},{1,17},{18,2},{2,18},{19,3},{3,19},{20,4},{4,... | collective-permute-start | bytes 393224 | tf_op jit(solution)/shard_map/ppermute | solution.py:15
  8.1 8.8 %collective-permute-start.2 = (bf16[64,10,1,128]{3,0,2,1:T(8,128)(2,1)S(1)}, bf16[64,10,1,128]{3,0,2,1:T(8,128)(2,1)S(1)}, u32[]{:S(2)}, u32[]{:S(2)}) collective-permute-start(bf16[64,10,1,128]{3,0,2,1:T(8,128)(2,1)S(1)} %get-tuple-element.14), channel_id=1, source_target_pairs={{0,1},{1,2},{2,3},{3,4},{4,5},{5,6},{6,7},{7,8},{8,9},{9,10},{10,1... | collective-permute-start | bytes 491528 | tf_op jit(solution)/shard_map/ppermute | solution.py:14
  8.2 8.7 %collective-permute-start.3 = (bf16[64,10,1,128]{3,0,2,1:T(8,128)(2,1)S(1)}, bf16[64,10,1,128]{3,0,2,1:T(8,128)(2,1)S(1)}, u32[]{:S(2)}, u32[]{:S(2)}) collective-permute-start(bf16[64,10,1,128]{3,0,2,1:T(8,128)(2,1)S(1)} %get-tuple-element.15), channel_id=1, source_target_pairs={{1,0},{2,1},{3,2},{4,3},{5,4},{6,5},{7,6},{8,7},{9,8},{10,9},{11,1... | collective-permute-start | bytes 491528 | tf_op jit(solution)/shard_map/ppermute | solution.py:15
  39.3 3.2 %copy-start.5 = (bf16[27,64,64]{2,1,0:T(8,128)(2,1)S(1)}, bf16[27,64,64]{2,1,0:T(8,128)(2,1)}, u32[]{:S(2)}) copy-start(bf16[27,64,64]{2,1,0:T(8,128)(2,1)} %param.8) | copy-start | bytes 663556
  39.3 3.2 %copy-start.7 = (pred[8,17]{0,1:T(8,128)(4,1)S(1)}, pred[8,17]{0,1:T(8,128)(4,1)}, u32[]{:S(2)}) copy-start(pred[8,17]{0,1:T(8,128)(4,1)} %constant.18) | copy-start | bytes 412
  186.7 0.8 copy-start.2
  188.3 2.4 collective-permute-start.4
  189.6 1.5 collective-permute-start.5
  197.2 8.3 %collective-permute-start.7 = (bf16[64,10,1,128]{3,0,2,1:T(8,128)(2,1)}, bf16[64,10,1,128]{3,0,2,1:T(8,128)(2,1)S(1)}, u32[]{:S(2)}, u32[]{:S(2)}) collective-permute-start(bf16[64,10,1,128]{3,0,2,1:T(8,128)(2,1)} %copy.32), channel_id=1, source_target_pairs={{1,0},{2,1},{3,2},{4,3},{5,4},{6,5},{7,6},{8,7},{9,8},{10,9},{11,1... | collective-permute-start | bytes 491528 | tf_op jit(solution)/shard_map/ppermute | solution.py:15
  202.0 8.4 %collective-permute-start.6 = (bf16[64,10,1,128]{3,0,2,1:T(8,128)(2,1)S(1)}, bf16[64,10,1,128]{3,0,2,1:T(8,128)(2,1)S(1)}, u32[]{:S(2)}, u32[]{:S(2)}) collective-permute-start(bf16[64,10,1,128]{3,0,2,1:T(8,128)(2,1)S(1)} %copy.31), channel_id=1, source_target_pairs={{0,1},{1,2},{2,3},{3,4},{4,5},{5,6},{6,7},{7,8},{8,9},{9,10},{10,1... | collective-permute-start | bytes 491528 | tf_op jit(solution)/shard_map/ppermute | solution.py:14
  211.9 1.3 copy-start.1
  234.7 3.2 %copy-start.3 = (f32[64]{0:T(128)S(1)}, f32[64]{0:T(128)}, u32[]{:S(2)}) copy-start(f32[64]{0:T(128)} %param.11) | copy-start | bytes 772
  234.7 3.2 %copy-start.8 = (pred[8,17]{0,1:T(8,128)(4,1)S(1)}, pred[8,17]{0,1:T(8,128)(4,1)}, u32[]{:S(2)}) copy-start(pred[8,17]{0,1:T(8,128)(4,1)} %constant.18) | copy-start | bytes 412
  248.4 1.4 copy-start.6
  254.0 3.7 %copy-start.4 = (f32[64]{0:T(128)S(1)}, f32[64]{0:T(128)}, u32[]{:S(2)}) copy-start(f32[64]{0:T(128)} %param.13) | copy-start | bytes 772
where the time goes:
time: 259 us
  matrix products  155 us (60%)
  local copies, waits for them, and re-layouts  63.9 us (25%)
  starting transfers between devices  14.6 us (6%)
  other arithmetic  12.6 us (5%)
  waiting for transfers between devices  11.6 us (4%)
    conv_general_dilated x2, matrix products, conv_layer(): lax.conv_general_dilated(padded[None], stencil, (1, 1, 1), 'VALID', dimen...  154 us
    conv_general_dilated x8, local copies, waits for them, and re-layouts, conv_layer(): lax.conv_general_dilated(padded[None], stencil, (1, 1, 1), 'VALID', dimen...  24.4 us
    unnamed x25, local copies, waits for them, and re-layouts  17.4 us
    ppermute x4, waiting for transfers between devices, extended(): before = lax.ppermute(last, axis, up)  10.6 us
    ppermute x4, starting transfers between devices, extended(): after = lax.ppermute(initial, axis, down)  9.94 us
    broadcast_in_dim x2, local copies, waits for them, and re-layouts, conv_layer(): padded[None]  8.92 us
    broadcast_in_dim x2, other arithmetic, conv_layer(): padded[None]  8.09 us
  transfers between devices with their start and end apart: 8, of which 6 were waited for; matrix products, arithmetic and copies ran while one was open for 2% of the time, Pallas kernels for 0%

commit v1 on v0

v1 whole, which is shorter than its diff:
```python
import jax
import jax.numpy as jnp
from jax import lax
from jax.experimental import pallas as pl
from jax.experimental.pallas import tpu as pltpu
from jax.sharding import PartitionSpec as P

BF = jnp.bfloat16
F32 = jnp.float32
WHOLE = pl.BlockSpec(memory_space=pltpu.VMEM)
TAPS = 9 * 64


def shape(*dims, kind=BF):
    return jax.ShapeDtypeStruct(dims, kind)


def kernel_call(body, outs, scratch, flops, name, *operands):
    size = lambda s: s.size * s.dtype.itemsize
    moved = sum(size(s) for s in operands) + sum(size(s) for s in outs)
    return pl.pallas_call(
        body,
        name=name,
        out_shape=outs,
        in_specs=[WHOLE] * len(operands),
        out_specs=[WHOLE] * len(outs),
        scratch_shapes=scratch,
        compiler_params=pltpu.CompilerParams(vmem_limit_bytes=28 * 2**20),
        cost_estimate=pl.CostEstimate(flops=flops, bytes_accessed=moved, transcendentals=0),
    )(*operands)


def lrelu(values):
    return jnp.maximum(values, 0.01 * values)


def shifted(dst, z, y, row):
    dst[z, y, 0:64] = pltpu.roll(row, 1, 1)
    dst[z, y, 64:128] = row
    dst[z, y, 128:192] = pltpu.roll(row, 127, 1)


def conv_pair(src, z, rows, weight, bias):
    cells = jnp.concatenate([src[z : z + 4, y : y + 3].reshape(4 * TAPS, 128) for y in rows], axis=1)
    sums = jnp.dot(weight[...], cells, preferred_element_type=F32)
    return lrelu(sums + bias[...]).astype(BF)


def split_kernel(vol, own, up, down, planes):
    for i, z in enumerate((6, 7, 0, 1, 2, 3, 4, 5)):
        rows = jnp.swapaxes(vol[:, z], 0, 1)
        own[z] = rows
        if i < 4:
            planes[i] = rows
        down[z] = rows[0:2]
        up[z] = rows[6:8]


def weight_kernel(first, first_bias, second, second_bias, third, third_bias, a1, a2, ad, b1, b2, bd, pick):
    eye = (lax.broadcasted_iota(jnp.int32, (64, 64), 0) == lax.broadcasted_iota(jnp.int32, (64, 64), 1))
    unit = eye.astype(BF)

    def flipped(rows):
        return lax.dot_general(unit, rows, (((1,), (1,)), ((), ())), preferred_element_type=F32).astype(BF)

    def column(bias):
        spread = jnp.where(eye, jnp.broadcast_to(bias[...].reshape(1, 64), (64, 64)), 0.0)
        return jnp.broadcast_to(jnp.sum(spread, axis=1, keepdims=True), (64, 256))

    blank = jnp.zeros((TAPS, 64), BF)
    for source, dest in ((first, a1), (second, a2)):
        rows = source[...].reshape(3 * TAPS, 64)
        dest[0:64] = flipped(jnp.concatenate([rows, blank], axis=0))
        dest[64:128] = flipped(jnp.concatenate([blank, rows], axis=0))
    ad[...] = flipped(third[...].reshape(512, 64))
    for source, dest in ((first_bias, b1), (second_bias, b2)):
        spread = column(source)
        dest[0:64] = spread
        dest[64:128] = spread
    bd[...] = column(third_bias)
    src = lax.broadcasted_iota(jnp.int32, (256, 256), 0)
    dst = lax.broadcasted_iota(jnp.int32, (256, 256), 1)
    half, cell = (dst // 64) % 2, dst % 64
    pick[...] = (src == half * 128 + 2 * cell + dst // 128).astype(F32).astype(BF)


def inner_kernel(own, planes, a1, b1, a2, b2, hidden, skip, vs, hs):
    for z in range(12):
        for y in range(8):
            row = own[z - 2, y] if 2 <= z < 10 else planes[z if z < 2 else z - 8, y]
            shifted(vs, z, y, row)
    for z in range(0, 10, 2):
        for y in range(0, 6, 2):
            out = conv_pair(vs, z, (y, y + 1), a1, b1)
            for i in range(2):
                for j in range(2):
                    row = out[64 * i : 64 * i + 64, 128 * j : 128 * j + 128]
                    shifted(hs, z + i, y + j, row)
                    place = {0: 0, 1: 1, 4: 2, 5: 3}.get(y + j)
                    if place is not None:
                        hidden[z + i, place] = row
    for z in range(0, 8, 2):
        for y in range(0, 4, 2):
            out = conv_pair(hs, z, (y, y + 1), a2, b2)
            for i in range(2):
                for j in range(2):
                    skip[z + i, y + j] = out[64 * i : 64 * i + 64, 128 * j : 128 * j + 128]


def outer_kernel(own, planes, above, below, corner_above, corner_below, hidden, mid, a1, b1, a2, b2, ad, bd, pick, skip, coarse, vs, hs, rows_out, cells):
    def source(z, y):
        if z < 2 or z >= 10:
            k = z if z < 2 else z - 8
            if y < 0:
                return corner_above[k, y + 2]
            if y >= 8:
                return corner_below[k, y - 8]
            return planes[k, y]
        if y < 0:
            return above[z - 2, y + 2]
        if y >= 8:
            return below[z - 2, y - 8]
        return own[z - 2, y]

    for strip in range(2):
        for z in range(12):
            for y in range(4):
                shifted(vs.at[strip], z, y, source(z, y - 2 if strip == 0 else y + 6))
    for strip in range(2):
        for z in range(10):
            for y in range(2):
                shifted(hs.at[strip], z, y + 2 * (1 - strip), hidden[z, 2 * strip + y])
    for strip in range(2):
        for z in range(0, 10, 2):
            out = conv_pair(vs.at[strip], z, (0, 1), a1, b1)
            for i in range(2):
                for j in range(2):
                    shifted(hs.at[strip], z + i, j + 2 * strip, out[64 * i : 64 * i + 64, 128 * j : 128 * j + 128])
    for z in range(8):
        for y in range(4):
            rows_out[z, y + 2] = mid[z, y]
    for strip in range(2):
        for z in range(0, 8, 2):
            out = conv_pair(hs.at[strip], z, (0, 1), a2, b2)
            for i in range(2):
                for j in range(2):
                    rows_out[z + i, 6 * strip + j] = out[64 * i : 64 * i + 64, 128 * j : 128 * j + 128]
    for z in range(8):
        skip[:, z] = jnp.swapaxes(rows_out[z], 0, 1)
    for z in range(8):
        for y in range(2):
            pair = rows_out[z, 4 * y : 4 * y + 4].reshape(256, 128)
            wide = jnp.concatenate([pair[0:128], pair[128:256]], axis=1)
            chosen = jnp.dot(wide, pick[...], preferred_element_type=F32).astype(BF)
            for p in range(2):
                for q in range(2):
                    cells[z, 2 * p + q, :, 128 * y : 128 * y + 128] = chosen[64 * p : 64 * p + 64, 128 * q : 128 * q + 128]
    found = []
    for z in range(4):
        sums = jnp.dot(ad[...], cells[2 * z : 2 * z + 2].reshape(512, 256), preferred_element_type=F32)
        found.append(lrelu(sums + bd[...]).astype(BF))
    for z in range(4):
        coarse[:, z] = found[z]


def per_device(volume, first_weight, first_bias, second_weight, second_bias, down_weight, down_bias):
    peers = lax.axis_size("filt")
    upward = [(i, (i + 1) % peers) for i in range(peers)]
    downward = [(j, i) for i, j in upward]
    swap = [(0, 1), (1, 0)]
    own, up, down, planes = kernel_call(
        split_kernel,
        [shape(8, 8, 64, 128), shape(8, 2, 64, 128), shape(8, 2, 64, 128), shape(4, 8, 64, 128)],
        [], 0, "split", volume,
    )
    planes = lax.ppermute(planes, "slab", swap)
    above = lax.ppermute(up, "filt", upward)
    below = lax.ppermute(down, "filt", downward)
    a1, a2, ad, b1, b2, bd, pick = kernel_call(
        weight_kernel,
        [shape(128, 4 * TAPS), shape(128, 4 * TAPS), shape(64, 512), shape(128, 256, kind=F32), shape(128, 256, kind=F32), shape(64, 256, kind=F32), shape(256, 256)],
        [], 10**8, "weights", first_weight, first_bias, second_weight, second_bias, down_weight, down_bias,
    )
    hidden, mid = kernel_call(
        inner_kernel,
        [shape(10, 4, 64, 128), shape(8, 4, 64, 128)],
        [pltpu.VMEM((12, 8, 192, 128), BF), pltpu.VMEM((10, 6, 192, 128), BF)],
        4 * 10**9, "inner", own, planes, a1, b1, a2, b2,
    )
    edges = lambda rows: jnp.concatenate([rows[6:8], rows[0:2]], axis=0)
    corner_above = lax.ppermute(edges(above), "slab", swap)
    corner_below = lax.ppermute(edges(below), "slab", swap)
    return kernel_call(
        outer_kernel,
        [shape(64, 8, 8, 128), shape(64, 4, 256)],
        [pltpu.VMEM((2, 12, 4, 192, 128), BF), pltpu.VMEM((2, 10, 4, 192, 128), BF), pltpu.VMEM((8, 8, 64, 128), BF), pltpu.VMEM((8, 4, 64, 256), BF)],
        4 * 10**9, "outer", own, planes, above, below, corner_above, corner_below, hidden, mid, a1, b1, a2, b2, ad, bd, pick,
    )


def solution(mesh):
    placed = (P("dp", "slab", "filt", None), P(), P(), P(), P(), P(), P())
    return jax.shard_map(
        lambda *args: tuple(per_device(*args)),
        mesh=mesh,
        in_specs=placed,
        out_specs=(P("dp", "slab", "filt", None), P("dp", "slab", "filt")),
        check_vma=False,
    )
```

time: 259 us -> 24.7 us (0.10)
  matrix products: 155 us -> 0 us
  local copies, waits for them, and re-layouts: 63.9 us -> 1.26 us
  other arithmetic: 12.6 us -> 0.03 us
  waiting for transfers between devices: 11.6 us -> 0.43 us
  Pallas kernels: 0 us -> 9.86 us
    conv_general_dilated x3 -> x0, matrix products: 155 us -> none  [the longest x2 154 us: conv_layer(): lax.conv_general_dilated(padded[None], stencil, (1, 1, 1), 'VALID', dimen...]
    conv_general_dilated x9 -> x0, local copies, waits for them, and re-layouts: 24.5 us -> none  [the longest x8 24.4 us: conv_layer(): lax.conv_general_dilated(padded[None], stencil, (1, 1, 1), 'VALID', dimen...]
    unnamed x25 -> x14, local copies, waits for them, and re-layouts: 17.4 us -> 1.24 us
    ppermute x8 -> x5, waiting for transfers between devices: 11.6 us -> 0.43 us  [the longest x1 0.42 us: per_device(): above = lax.ppermute(up, 'filt', upward)]
    pallas_call x0 -> x4, Pallas kernels: none -> 9.86 us  [kernel_call(): pl.pallas_call(body, name=name, out_shape=outs, in_specs=[WHOLE] * len(op...]
    broadcast_in_dim x2 -> x0, local copies, waits for them, and re-layouts: 8.92 us -> none  [conv_layer(): padded[None]]
    broadcast_in_dim x2 -> x0, other arithmetic: 8.09 us -> none  [conv_layer(): padded[None]]
    slice x8 -> x2, local copies, waits for them, and re-layouts: 8.03 us -> 0.02 us  [per_device(): edges = lambda rows: jnp.concatenate([rows[6:8], rows[0:2]], axis=0)]
  transfers between devices with their start and end apart: 8 -> 5, of which waited for: 6 -> 1; matrix products, arithmetic and copies ran while one was open for 2% -> 0% of each run, Pallas kernels for 0% -> 19%
where the time goes in v1:
time: 24.7 us; the launch traced here: 24.5 us
  starting transfers between devices  12.2 us (49%)
  Pallas kernels  9.86 us (40%)
  local copies, waits for them, and re-layouts  1.26 us (5%)
  between operations  0.72 us (3%)
  waiting for transfers between devices  0.43 us (2%)
    pallas_call x4, Pallas kernels, kernel_call(): pl.pallas_call(body, name=name, out_shape=outs, in_specs=[WHOLE] * len(op...  9.86 us
    ppermute x1, starting transfers between devices, per_device(): below = lax.ppermute(down, 'filt', downward)  3.84 us
    ppermute x1, starting transfers between devices, per_device(): corner_above = lax.ppermute(edges(above), 'slab', swap)  3.27 us
    ppermute x1, starting transfers between devices, per_device(): planes = lax.ppermute(planes, 'slab', swap)  2.71 us
    ppermute x1, starting transfers between devices, per_device(): above = lax.ppermute(up, 'filt', upward)  2.12 us
    unnamed x14, local copies, waits for them, and re-layouts  1.24 us
  transfers between devices with their start and end apart: 5, of which 1 were waited for; matrix products, arithmetic and copies ran while one was open for 0% of the time, Pallas kernels for 19%

profile of v1, /device:TPU:1, one launch (start us, length us, event | category | flops | bytes accessed | tf_op | source)
XLA Modules:
  0.0 24.5 jit_solution(12852807273609279248)
XLA Ops:
  0.6 0.0 copy-start
  0.6 1.2 %copy-done = bf16[64,8,8,128]{3,2,1,0:T(8,128)(2,1)S(1)} copy-done((bf16[64,8,8,128]{3,2,1,0:T(8,128)(2,1)S(1)}, bf16[64,8,8,128]{3,2,1,0:T(8,128)(2,1)}, u32[]{:S(2)}) %copy-start) | copy-done | bytes 1048600
  1.9 0.0 copy-start.1
  1.9 0.0 copy-start.2
  1.9 0.5 %split.1 = (bf16[8,8,64,128]{3,2,1,0:T(8,128)(2,1)S(1)}, bf16[8,2,64,128]{3,2,1,0:T(8,128)(2,1)S(1)}, bf16[8,2,64,128]{3,2,1,0:T(8,128)(2,1)S(1)}, bf16[4,8,64,128]{3,2,1,0:T(8,128)(2,1)S(1)}) custom-call(bf16[64,8,8,128]{3,2,1,0:T(8,128)(2,1)S(1)} %copy-done), custom_call_target="tpu_custom_call" | custom-call | bytes 3145728 | tf_op jit(solution)/shard_map/split/pallas_call | solution.py:21
  2.3 2.1 %collective-permute-start.1 = (bf16[8,2,64,128]{3,2,1,0:T(8,128)(2,1)S(1)}, bf16[8,2,64,128]{3,2,1,0:T(8,128)(2,1)S(1)}, u32[]{:S(2)}, u32[]{:S(2)}) collective-permute-start(bf16[8,2,64,128]{3,2,1,0:T(8,128)(2,1)S(1)} %get-tuple-element.17), channel_id=1, source_target_pairs={{0,1},{1,2},{2,3},{3,4},{4,5},{5,6},{6,7},{7,8},{8,9},{9,10},{10,1... | collective-permute-start | bytes 786440 | tf_op jit(solution)/shard_map/ppermute | solution.py:177
  4.5 3.8 %collective-permute-start.2 = (bf16[8,2,64,128]{3,2,1,0:T(8,128)(2,1)S(1)}, bf16[8,2,64,128]{3,2,1,0:T(8,128)(2,1)S(1)}, u32[]{:S(2)}, u32[]{:S(2)}) collective-permute-start(bf16[8,2,64,128]{3,2,1,0:T(8,128)(2,1)S(1)} %get-tuple-element.18), channel_id=1, source_target_pairs={{1,0},{2,1},{3,2},{4,3},{5,4},{6,5},{7,6},{8,7},{9,8},{10,9},{11,1... | collective-permute-start | bytes 786440 | tf_op jit(solution)/shard_map/ppermute | solution.py:178
  8.3 2.7 %collective-permute-start = (bf16[4,8,64,128]{3,2,1,0:T(8,128)(2,1)S(1)}, bf16[4,8,64,128]{3,2,1,0:T(8,128)(2,1)S(1)}, u32[]{:S(2)}, u32[]{:S(2)}) collective-permute-start(bf16[4,8,64,128]{3,2,1,0:T(8,128)(2,1)S(1)} %get-tuple-element.16), channel_id=1, source_target_pairs={{0,16},{16,0},{1,17},{17,1},{2,18},{18,2},{3,19},{19,3},{4,20},{20... | collective-permute-start | bytes 1572872 | tf_op jit(solution)/shard_map/ppermute | solution.py:176
  11.0 0.0 copy-done.1
  11.0 0.0 copy-done.2
  11.0 0.0 copy-done.3
  11.0 0.0 copy-done.4
  11.0 0.0 copy-done.5
  11.0 0.0 copy-done.6
  11.0 0.8 %weights.1 = (bf16[128,2304]{1,0:T(8,128)(2,1)S(1)}, bf16[128,2304]{1,0:T(8,128)(2,1)S(1)}, bf16[64,512]{1,0:T(8,128)(2,1)S(1)}, f32[128,256]{1,0:T(8,128)S(1)},...) custom-call(bf16[27,64,64]{2,1,0:T(8,128)(2,1)S(1)} %copy-done.1, f32[64]{0:T(128)S(1)} %copy-done.4, ...), custom_call_target="tpu_custom_call" | custom-call | flops 100000000 | bytes 2212608 | tf_op jit(solution)/shard_map/weights/pallas_call | solution.py:21
  11.8 0.4 %collective-permute-done.1.above = bf16[8,2,64,128]{3,2,1,0:T(8,128)(2,1)S(1)} collective-permute-done((bf16[8,2,64,128]{3,2,1,0:T(8,128)(2,1)S(1)}, bf16[8,2,64,128]{3,2,1,0:T(8,128)(2,1)S(1)}, u32[]{:S(2)}, u32[]{:S(2)}) %collective-permute-start.1) | collective-permute-done | bytes 262176 | tf_op jit(solution)/shard_map/ppermute | solution.py:177
  12.3 3.3 %collective-permute-start.3 = (bf16[4,2,64,128]{3,2,1,0:T(8,128)(2,1)S(1)}, bf16[4,2,64,128]{3,2,1,0:T(8,128)(2,1)S(1)}, u32[]{:S(2)}, u32[]{:S(2)}) collective-permute-start(bf16[4,2,64,128]{3,2,1,0:T(8,128)(2,1)S(1)} %pad_maximum_fusion), channel_id=1, source_target_pairs={{0,16},{16,0},{1,17},{17,1},{2,18},{18,2},{3,19},{19,3},{4,20},{20... | collective-permute-start | bytes 393224 | tf_op jit(solution)/shard_map/ppermute | solution.py:191
  15.5 0.0 collective-permute-done.2.below
  15.6 0.3 %collective-permute-start.4 = (bf16[4,2,64,128]{3,2,1,0:T(8,128)(2,1)S(1)}, bf16[4,2,64,128]{3,2,1,0:T(8,128)(2,1)S(1)}, u32[]{:S(2)}, u32[]{:S(2)}) collective-permute-start(bf16[4,2,64,128]{3,2,1,0:T(8,128)(2,1)S(1)} %pad_maximum_fusion.1), channel_id=1, source_target_pairs={{0,16},{16,0},{1,17},{17,1},{2,18},{18,2},{3,19},{19,3},{4,20},{20... | collective-permute-start | bytes 393224 | tf_op jit(solution)/shard_map/ppermute | solution.py:192
  15.9 0.0 collective-permute-done.planes
  15.9 4.0 %inner.1 = (bf16[10,4,64,128]{3,2,1,0:T(8,128)(2,1)S(1)}, bf16[8,4,64,128]{3,2,1,0:T(8,128)(2,1)S(1)}) custom-call(bf16[8,8,64,128]{3,2,1,0:T(8,128)(2,1)S(1)} %get-tuple-element.15.own, bf16[4,8,64,128]{3,2,1,0:T(8,128)(2,1)S(1)} %collective-permute-done.planes, bf16[128,2304]{1,0:T(8,128)(2,1)S(1)} %get-tuple-element.19.a1, ...), custom_call_target="tpu_custom_call" | custom-call | flops 4000000000 | bytes 4194304 | tf_op jit(solution)/shard_map/inner/pallas_call | solution.py:21
  19.9 0.0 collective-permute-done.3.corner_above
  19.9 0.0 collective-permute-done.4.corner_below
  19.9 4.7 %outer.1 = (bf16[64,8,8,128]{3,2,1,0:T(8,128)(2,1)}, bf16[64,4,256]{2,1,0:T(4,128)(2,1)}) custom-call(bf16[8,8,64,128]{3,2,1,0:T(8,128)(2,1)S(1)} %get-tuple-element.15.own, bf16[4,8,64,128]{3,2,1,0:T(8,128)(2,1)S(1)} %collective-permute-done.planes, bf16[8,2,64,128]{3,2,1,0:T(8,128)(2,1)S(1)} %collective-permute-done.1.above, ...), custom_call_target="tpu_custom_call" | custom-call | flops 4000000000 | bytes 6422528 | tf_op jit(solution)/shard_map/outer/pallas_call | solution.py:21
  (8 shorter events, 0.1 us)
Async XLA Ops:
  0.6 1.2 %copy-start = (bf16[64,8,8,128]{3,2,1,0:T(8,128)(2,1)S(1)}, bf16[64,8,8,128]{3,2,1,0:T(8,128)(2,1)}, u32[]{:S(2)}) copy-start(bf16[64,8,8,128]{3,2,1,0:T(8,128)(2,1)} %vol.1) | copy-start | bytes 3145732
  1.9 9.1 %copy-start.1 = (bf16[27,64,64]{2,1,0:T(8,128)(2,1)S(1)}, bf16[27,64,64]{2,1,0:T(8,128)(2,1)}, u32[]{:S(2)}) copy-start(bf16[27,64,64]{2,1,0:T(8,128)(2,1)} %first.1) | copy-start | bytes 663556
  1.9 9.1 %copy-start.2 = (bf16[27,64,64]{2,1,0:T(8,128)(2,1)S(1)}, bf16[27,64,64]{2,1,0:T(8,128)(2,1)}, u32[]{:S(2)}) copy-start(bf16[27,64,64]{2,1,0:T(8,128)(2,1)} %second.1) | copy-start | bytes 663556
  1.9 9.1 %copy-start.3 = (bf16[8,64,64]{2,1,0:T(8,128)(2,1)S(1)}, bf16[8,64,64]{2,1,0:T(8,128)(2,1)}, u32[]{:S(2)}) copy-start(bf16[8,64,64]{2,1,0:T(8,128)(2,1)} %third.1) | copy-start | bytes 196612
  2.3 9.9 %collective-permute-start.1 = (bf16[8,2,64,128]{3,2,1,0:T(8,128)(2,1)S(1)}, bf16[8,2,64,128]{3,2,1,0:T(8,128)(2,1)S(1)}, u32[]{:S(2)}, u32[]{:S(2)}) collective-permute-start(bf16[8,2,64,128]{3,2,1,0:T(8,128)(2,1)S(1)} %get-tuple-element.17), channel_id=1, source_target_pairs={{0,1},{1,2},{2,3},{3,4},{4,5},{5,6},{6,7},{7,8},{8,9},{9,10},{10,1... | collective-permute-start | bytes 786440 | tf_op jit(solution)/shard_map/ppermute | solution.py:177
  4.4 6.6 %copy-start.4 = (f32[64]{0:T(128)S(1)}, f32[64]{0:T(128)}, u32[]{:S(2)}) copy-start(f32[64]{0:T(128)} %first_bias.1) | copy-start | bytes 772
  4.4 6.6 %copy-start.5 = (f32[64]{0:T(128)S(1)}, f32[64]{0:T(128)}, u32[]{:S(2)}) copy-start(f32[64]{0:T(128)} %second_bias.1) | copy-start | bytes 772
  4.4 6.6 %copy-start.6 = (f32[64]{0:T(128)S(1)}, f32[64]{0:T(128)}, u32[]{:S(2)}) copy-start(f32[64]{0:T(128)} %third_bias.1) | copy-start | bytes 772
  4.5 11.1 %collective-permute-start.2 = (bf16[8,2,64,128]{3,2,1,0:T(8,128)(2,1)S(1)}, bf16[8,2,64,128]{3,2,1,0:T(8,128)(2,1)S(1)}, u32[]{:S(2)}, u32[]{:S(2)}) collective-permute-start(bf16[8,2,64,128]{3,2,1,0:T(8,128)(2,1)S(1)} %get-tuple-element.18), channel_id=1, source_target_pairs={{1,0},{2,1},{3,2},{4,3},{5,4},{6,5},{7,6},{8,7},{9,8},{10,9},{11,1... | collective-permute-start | bytes 786440 | tf_op jit(solution)/shard_map/ppermute | solution.py:178
  8.3 7.6 %collective-permute-start = (bf16[4,8,64,128]{3,2,1,0:T(8,128)(2,1)S(1)}, bf16[4,8,64,128]{3,2,1,0:T(8,128)(2,1)S(1)}, u32[]{:S(2)}, u32[]{:S(2)}) collective-permute-start(bf16[4,8,64,128]{3,2,1,0:T(8,128)(2,1)S(1)} %get-tuple-element.16), channel_id=1, source_target_pairs={{0,16},{16,0},{1,17},{17,1},{2,18},{18,2},{3,19},{19,3},{4,20},{20... | collective-permute-start | bytes 1572872 | tf_op jit(solution)/shard_map/ppermute | solution.py:176
  12.3 7.6 %collective-permute-start.3 = (bf16[4,2,64,128]{3,2,1,0:T(8,128)(2,1)S(1)}, bf16[4,2,64,128]{3,2,1,0:T(8,128)(2,1)S(1)}, u32[]{:S(2)}, u32[]{:S(2)}) collective-permute-start(bf16[4,2,64,128]{3,2,1,0:T(8,128)(2,1)S(1)} %pad_maximum_fusion), channel_id=1, source_target_pairs={{0,16},{16,0},{1,17},{17,1},{2,18},{18,2},{3,19},{19,3},{4,20},{20... | collective-permute-start | bytes 393224 | tf_op jit(solution)/shard_map/ppermute | solution.py:191
  15.6 4.3 %collective-permute-start.4 = (bf16[4,2,64,128]{3,2,1,0:T(8,128)(2,1)S(1)}, bf16[4,2,64,128]{3,2,1,0:T(8,128)(2,1)S(1)}, u32[]{:S(2)}, u32[]{:S(2)}) collective-permute-start(bf16[4,2,64,128]{3,2,1,0:T(8,128)(2,1)S(1)} %pad_maximum_fusion.1), channel_id=1, source_target_pairs={{0,16},{16,0},{1,17},{17,1},{2,18},{18,2},{3,19},{19,3},{4,20},{20... | collective-permute-start | bytes 393224 | tf_op jit(solution)/shard_map/ppermute | solution.py:192
